TPU v7x, 32 devices: a whole 2x2x4 slice. The times are simulated.
32 devices in a mesh: gx: 4 (over y, x), gy: 2 (over core), gz: 4 (over z).
Axes of the slice: x: 2, y: 2, z: 4, core: 2. Of those that a mesh axis runs over, the one named last changes fastest.
Arguments:
- populations: float32 [19, 64, 32, 512], P(None, 'gz', 'gy', 'gx'), may hold values from 0.25 to 21, as said below
- solute_state: float32 [7, 256, 4096], P(None, ('gx', 'gy', 'gz')), may hold values from 0.05 to 3.9, as said below
- pore_mask: int32 [64, 32, 512], P('gz', 'gy', 'gx'), may hold values from 0 to 1, as said below
- block_slot: int32 [4, 2, 32], P('gz', 'gy', 'gx'), may hold values from -1 to 31, as said below
- slot_block: int32 [256], P(('gx', 'gy', 'gz')), may hold values from -1 to 31, as said below
Outputs:
- new_populations: float32 [19, 64, 32, 512], P(None, 'gz', 'gy', 'gx')
- new_solute: float32 [7, 256, 4096], P(None, ('gx', 'gy', 'gz'))
Inputs may be any that keep to these rules, and one draw needn't show every extreme that they name: pore_mask is 1 only inside blocks listed in block_slot. `block_slot`: in each column of fixed gx and gy, the listed blocks are numbered k = 0, 1, ... in order of the gz index and then of the x block within the device; block k sits in owner k % 4 (index along gz within the same column), slot k // 4. Every device lists 1 to 8 blocks and in every column some device lists all 8, so one device hands 2 blocks to some owner. `slot_block`: the inverse of block_slot: an owner's filled slots come first, in increasing k. `populations`: Positive. `solute_state`: Positive.
All inputs are finite; a program needn't handle non-finite values.
Results may differ from a plain program's by a relative error of at most 0.0001.
Values sent between devices are 32-bit elements; how exact they have to be, the bound alone decides.
A program may use at most 192 MiB of HBM per device.

v0:
```python
import functools

import jax
import jax.numpy as jnp
from jax import lax
from jax.experimental import pallas as pl
from jax.experimental.pallas import tpu as pltpu
from jax.sharding import PartitionSpec as P

STEPS = 4
AXES = ("gx", "gy", "gz")

FLOW_DIRS = [
    (0, 0, 0),
    (1, 0, 0),
    (-1, 0, 0),
    (0, 1, 0),
    (0, -1, 0),
    (0, 0, 1),
    (0, 0, -1),
    (1, 1, 0),
    (-1, -1, 0),
    (1, -1, 0),
    (-1, 1, 0),
    (1, 0, 1),
    (-1, 0, -1),
    (1, 0, -1),
    (-1, 0, 1),
    (0, 1, 1),
    (0, -1, -1),
    (0, 1, -1),
    (0, -1, 1),
]
FLOW_WEIGHTS = [1.0 / 3.0] + [1.0 / 18.0] * 6 + [1.0 / 36.0] * 12
OPP = [FLOW_DIRS.index((-a, -b, -c)) for a, b, c in FLOW_DIRS]
OMEGA_FLOW = 1.2
OMEGA_SOLUTE = 1.5
FORCE_GAIN = 0.02
REST_CONC = 8.0
SIGNS = (1, -1)

X_SIDE = [[FLOW_DIRS.index((s, b, c)) for b, c in ((0, 0), (1, 0), (-1, 0), (0, 1), (0, -1))] for s in SIGNS]
Y_SIDE = [[FLOW_DIRS.index((a, s, c)) for a, c in ((0, 0), (1, 0), (-1, 0), (0, 1), (0, -1))] for s in SIGNS]
Z_SIDE = [[FLOW_DIRS.index((a, b, s)) for a, b in ((0, 0), (1, 0), (-1, 0), (0, 1), (0, -1))] for s in SIGNS]
X_OFFS = [(0, 0), (1, 0), (-1, 0), (0, 1), (0, -1)]


def side(sign):
    return 0 if sign > 0 else 1


def iota(axis, shape=(16, 128)):
    return lax.broadcasted_iota(jnp.int32, shape, axis)


def swap_chunks(v):
    sub = iota(0, (8, 128))
    chunk = lax.shift_right_logical(iota(1, (8, 128)), 4)
    for k in (1, 2, 4):
        sbit = (sub & k) != 0
        if k == 4:
            both = pltpu.roll(pltpu.roll(v, 64, 1), 4, 0)
            v = jnp.where(((sub ^ chunk) & k) == 0, v, both)
        else:
            up = pltpu.roll(pltpu.roll(v, 16 * k, 1), 8 - k, 0)
            down = pltpu.roll(pltpu.roll(v, 128 - 16 * k, 1), k, 0)
            same = ((sub ^ chunk) & k) == 0
            v = jnp.where(same, v, jnp.where(sbit, down, up))
    return v


def kernel(
    sizes, cap, pop_ref, sol_ref, mask_ref, bs_ref, sb_ref, out_pop, out_sol,
    F, G, S, U, B, XM, YM, ZM, XH, YH, YE, ZH, XC, YC, SM, SH,
    T, stage, recv, stage2, recv2,
    f_send, f_recv, s_send, s_recv, a_send, a_recv, b_send, b_recv, own_sem,
):
    n_x, n_y, n_z = sizes
    me = tuple(lax.axis_index(a) for a in AXES)
    lane = iota(1)
    row = iota(0)
    size_z = mask_ref.shape[0]
    slots = sb_ref.shape[0]
    tiles = bs_ref.shape[2]
    comps = sol_ref.shape[0]

    def exists(off):
        ok = None
        for pos, n, o in zip(me, sizes, off):
            if o == 0:
                continue
            c = (pos + o < n) if o > 0 else (pos >= 1)
            ok = c if ok is None else jnp.logical_and(ok, c)
        return ok

    def dev(off):
        return {a: p + o for a, p, o in zip(AXES, me, off)}

    neighbours = [c for c in FLOW_DIRS[1:]]

    XH[0] = jnp.zeros_like(XH[0])
    YH[0] = jnp.zeros_like(YH[0])
    YE[0] = jnp.zeros_like(YE[0])
    ZH[0] = jnp.zeros_like(ZH[0])

    barrier = pltpu.get_barrier_semaphore()
    count = jnp.int32(n_z - 1)
    for off in neighbours:
        if off[0] == 0 and off[1] == 0:
            continue
        ok = exists(off)
        count = count + ok.astype(jnp.int32)

        @pl.when(ok)
        def _(off=off):
            pl.semaphore_signal(barrier, inc=1, device_id=dev(off), device_id_type=pl.DeviceIdType.MESH)

    for k in range(1, n_z):
        other = lax.rem(me[2] + k, n_z)
        pl.semaphore_signal(
            barrier, inc=1, device_id={"gx": me[0], "gy": me[1], "gz": other},
            device_id_type=pl.DeviceIdType.MESH)

    def routing(values, per):
        group = [lax.div(jnp.maximum(v, 0), jnp.int32(per)) for v in values]
        held = [(v >= 0).astype(jnp.int32) for v in values]
        rank = []
        for s in range(len(values)):
            r = jnp.int32(0)
            for e in range(s):
                r = r + jnp.where(group[e] == group[s], held[e], 0)
            rank.append(r)
        pick = []
        for g in range(n_z):
            for p in range(cap):
                at = jnp.int32(0)
                for s in range(len(values)):
                    hit = jnp.logical_and(group[s] == g, rank[s] == p)
                    at = at + jnp.where(hit, held[s] * s, 0)
                pick.append(at)
        where = [(group[s] * cap + rank[s] + 1) * held[s] - 1 for s in range(len(values))]
        return pick, where

    slot_pick, slot_where = routing([sb_ref[s] for s in range(slots)], tiles)
    tile_pick, tile_where = routing([bs_ref[0, 0, j] for j in range(tiles)], slots)
    rows = T.shape[1] // slots

    def blocks_of(c, n):
        return [T[c, k * rows:(k + 1) * rows, :] for k in range(n)]

    def pairs_of(buf, c):
        return [buf[q // cap, q % cap, c] for q in range(n_z * cap)]

    def choose(index, options):
        at = jnp.full(options[0].shape, index, jnp.int32)
        out = jnp.zeros_like(options[0])
        for k, v in enumerate(options):
            out = jnp.where(at == k, v, out)
        return out

    def gather(c, _):
        for r in range(rows):
            T[c, pl.ds(r, slots, stride=rows), :] = sol_ref[c, :, r * 128:(r + 1) * 128]
        for q in range(n_z * cap):
            stage[q // cap, q % cap, c] = choose(slot_pick[q], blocks_of(c, slots))
        return 0

    lax.fori_loop(0, comps, gather, 0)
    pl.semaphore_wait(barrier, count)

    def exchange_blocks(src, dst, send, rec, own):
        copies = []
        for k in range(1, n_z):
            other = lax.rem(me[2] + k, n_z)
            copies.append(pltpu.make_async_remote_copy(
                src_ref=src.at[other], dst_ref=dst.at[me[2]],
                send_sem=send.at[k], recv_sem=rec.at[k],
                device_id={"gx": me[0], "gy": me[1], "gz": other},
                device_id_type=pl.DeviceIdType.MESH))
        for c in copies:
            c.start()
        mine = pltpu.make_async_copy(src.at[me[2]], dst.at[me[2]], own)
        mine.start()
        return copies + [mine]

    moving = exchange_blocks(stage, recv, a_send, a_recv, own_sem.at[0])

    def flow_messages(slot):
        out = []
        for si, s in enumerate(SIGNS):
            for m, (oy, oz) in enumerate(X_OFFS):
                out.append(((s, oy, oz), XM.at[si], XH.at[slot, si, m]))
        for si, s in enumerate(SIGNS):
            out.append(((0, s, 0), YM.at[si], YH.at[slot, si]))
            for zi, z in enumerate(SIGNS):
                src = YM.at[si, 3 + zi, pl.ds(size_z - 8 if z > 0 else 0, 8)]
                out.append(((0, s, z), src, YE.at[slot, si, zi]))
        for si, s in enumerate(SIGNS):
            out.append(((0, 0, s), ZM.at[si], ZH.at[slot, si]))
        return out

    def solute_messages():
        out = []
        for ax in range(3):
            for si, s in enumerate(SIGNS):
                off = tuple(s if a == ax else 0 for a in range(3))
                out.append((off, SM.at[ax, si], SH.at[ax, si]))
        return out

    def exchange(messages, send, rec):
        copies = []
        for k, (off, src, dst) in enumerate(messages):
            copy = pltpu.make_async_remote_copy(
                src_ref=src, dst_ref=dst, send_sem=send.at[k], recv_sem=rec(k),
                device_id=dev(off), device_id_type=pl.DeviceIdType.MESH)
            copies.append(copy)

            @pl.when(exists(off))
            def _(copy=copy):
                copy.start()

        def finish():
            for (off, _, _), copy in zip(messages, copies):
                back = tuple(-o for o in off)

                @pl.when(exists(back))
                def _(copy=copy):
                    copy.wait_recv()
            for (off, _, _), copy in zip(messages, copies):
                @pl.when(exists(off))
                def _(copy=copy):
                    copy.wait_send()
        return finish

    def pack_x(z, planes, acc):
        new = []
        at_z = (lane & 15) == z
        for si, s in enumerate(SIGNS):
            w = None
            for j, v in enumerate(planes[si]):
                r = pltpu.roll(v, 16 * j + 1 if s > 0 else 16 * j, 1) if (s > 0 or j) else v
                w = r if w is None else jnp.where((lane >= 16 * j), r, w)
            new.append(jnp.where(at_z, pltpu.roll(w, z, 1), acc[si]))
        return tuple(new)

    def pack_flow(z, values, acc):
        for si, s in enumerate(SIGNS):
            e = 15 if s > 0 else 0
            for j, d in enumerate(Y_SIDE[si]):
                YM[si, j, pl.ds(z, 1), :] = values[d][e:e + 1, :]
        return pack_x(z, [[values[d] for d in X_SIDE[si]] for si in range(2)], acc)

    def finish_pack(acc):
        for si, s in enumerate(SIGNS):
            XM[si] = acc[si]
            for j, d in enumerate(Z_SIDE[si]):
                ZM[si, j] = F[d, size_z if s > 0 else 1]

    zero2 = (jnp.zeros((16, 128), jnp.float32),) * 2

    def flow_halo(slot):
        for si, s in enumerate(SIGNS):
            for j, d in enumerate(Z_SIDE[si]):
                F[d, 0 if s > 0 else size_z + 1] = ZH[slot, si, j]
            for zi, z in enumerate(SIGNS):
                base = YH[slot, si, 3 + zi]
                e = YE[slot, si, zi, 7:8, :] if z > 0 else YE[slot, si, zi, 0:1, :]
                edge = row == (15 if z > 0 else 0)
                YC[si, zi] = pltpu.roll(jnp.where(edge, jnp.broadcast_to(e, (16, 128)), base), 1 if z > 0 else 15, 0)
            base = XH[slot, si, 0]
            g1 = pltpu.roll(jnp.where(row == 15, XH[slot, si, 1], base), 1, 0)
            g2 = pltpu.roll(jnp.where(row == 0, XH[slot, si, 2], base), 15, 0)
            g3 = jnp.where(lane == 48, pltpu.roll(XH[slot, si, 3], 113, 1), pltpu.roll(base, 1, 1))
            g4 = jnp.where(lane == 79, pltpu.roll(XH[slot, si, 4], 15, 1), pltpu.roll(base, 127, 1))
            c = jnp.where(lane < 16, base, g1)
            c = jnp.where(lane < 32, c, g2)
            c = jnp.where(lane < 48, c, g3)
            XC[si] = jnp.where(lane < 64, c, g4)

    def shifted_flow(slot, z, xz):
        out = [None]
        for d in range(1, 19):
            cx, cy, cz = FLOW_DIRS[d]
            v = F[d, z + (1 - cz)]
            if cy:
                si = side(cy)
                j = Y_SIDE[si].index(d)
                if j < 3:
                    e = YH[slot, si, j, pl.ds(z, 1), :]
                else:
                    e = YC[si, j - 3, pl.ds(z, 1), :]
                v = jnp.where(row == (0 if cy > 0 else 15), jnp.broadcast_to(e, (16, 128)),
                              pltpu.roll(v, 1 if cy > 0 else 15, 0))
            if cx:
                si = side(cx)
                j = X_SIDE[si].index(d)
                if cx > 0:
                    h = pltpu.roll(xz[0], 128 - 16 * j, 1) if j else xz[0]
                    v = jnp.where(lane == 0, h, pltpu.roll(v, 1, 1))
                else:
                    h = pltpu.roll(xz[1], 127 - 16 * j, 1)
                    v = jnp.where(lane == 127, h, pltpu.roll(v, 127, 1))
            out.append(v)
        return out

    def x_planes(refs, z):
        back = lax.rem(128 - z, 128)
        return [pltpu.roll(r, back, 1) for r in refs]

    def moments(z, p, porous):
        density = p[0]
        for v in p[1:]:
            density = density + v
        inv = porous / density
        m = []
        for ax in range(3):
            total = None
            for d in range(1, 19):
                if FLOW_DIRS[d][ax] > 0:
                    diff = p[d] - p[OPP[d]]
                    total = diff if total is None else total + diff
            m.append(total * inv)
        U[0, z] = density
        for ax in range(3):
            U[1 + ax, z] = m[ax]

    def fill(z, acc):
        porous = mask_ref[z].astype(jnp.float32)
        for d in range(19):
            F[d, z + 1] = porous
        p = [pop_ref[d, z] for d in range(19)]
        for d in range(19):
            out_pop[d, z] = p[d]
        moments(z, p, porous)
        return pack_flow(z, [porous] * 19, acc)

    finish_pack(lax.fori_loop(0, size_z, fill, zero2))
    exchange(flow_messages(0), f_send, lambda k: f_recv.at[0, k])()
    flow_halo(0)

    def link_bits(z, _):
        xz = x_planes([XC[0], XC[1]], z)
        moved = shifted_flow(0, z, xz)
        pore = mask_ref[z] > 0
        bits = jnp.where(pore, 1, 0)
        for d in range(1, 19):
            bits = bits | jnp.where(jnp.logical_and(pore, moved[d] > 0.5), 1 << d, 0)
        B[z] = bits
        return 0

    lax.fori_loop(0, size_z, link_bits, 0)

    for c in moving:
        c.wait()

    def place(c, _):
        for j in range(tiles):
            T[c, j * rows:(j + 1) * rows, :] = choose(tile_where[j], pairs_of(recv, c))
        for r in range(rows):
            v = T[c, pl.ds(r, tiles, stride=rows), :]
            G[c, r // 2, (r % 2) * 8:(r % 2) * 8 + 8, :] = swap_chunks(v)
        return 0

    lax.fori_loop(0, comps, place, 0)

    def unplace(c, _):
        for r in range(rows):
            T[c, pl.ds(r, tiles, stride=rows), :] = swap_chunks(G[c, r // 2, (r % 2) * 8:(r % 2) * 8 + 8, :])
        for q in range(n_z * cap):
            stage2[q // cap, q % cap, c] = choose(tile_pick[q], blocks_of(c, tiles))
        return 0

    def collide_solute(z, acc):
        g = [G[i, z] for i in range(7)]
        u = [U[1 + a, z] for a in range(3)]
        conc = g[0]
        for v in g[1:]:
            conc = conc + v
        post = [g[0] * (1 - OMEGA_SOLUTE) + (OMEGA_SOLUTE * 0.25) * conc]
        cw = (OMEGA_SOLUTE * 0.125) * conc
        for i in range(1, 7):
            ax = (i - 1) // 2
            f = 1.0 + 4.0 * u[ax] if i % 2 else 1.0 - 4.0 * u[ax]
            post.append(g[i] * (1 - OMEGA_SOLUTE) + cw * f)
        for i in range(7):
            S[i, z + 1] = post[i]
        SM[1, 0, pl.ds(z, 1), :] = post[3][15:16, :]
        SM[1, 1, pl.ds(z, 1), :] = post[4][0:1, :]
        at_z = lane == z
        return (jnp.where(at_z, pltpu.roll(post[1], z + 1, 1), acc[0]),
                jnp.where(at_z, pltpu.roll(post[2], z, 1), acc[1]))

    def stream_solute_collide_flow(z, acc):
        bits = B[z]
        pore = (bits & 1) != 0
        xz = x_planes([SH[0, 0], SH[0, 1]], z)
        s = [S[i, z + 1] for i in range(7)]
        new = [s[0]]
        for i in range(1, 7):
            cx, cy, cz = FLOW_DIRS[i]
            if cx > 0:
                v = jnp.where(lane == 0, xz[0], pltpu.roll(s[i], 1, 1))
            elif cx < 0:
                v = jnp.where(lane == 127, pltpu.roll(xz[1], 127, 1), pltpu.roll(s[i], 127, 1))
            elif cy:
                e = SH[1, side(cy), pl.ds(z, 1), :]
                v = jnp.where(row == (0 if cy > 0 else 15), jnp.broadcast_to(e, (16, 128)),
                              pltpu.roll(s[i], 1 if cy > 0 else 15, 0))
            else:
                v = S[i, z + (1 - cz)]
            new.append(jnp.where((bits & (1 << i)) != 0, v, jnp.where(pore, s[OPP[i]], s[i])))
        conc = new[0]
        for v in new[1:]:
            conc = conc + v
        for i in range(7):
            G[i, z] = new[i]
        rho = U[0, z]
        ux = U[1, z]
        uy = U[2, z]
        uz = U[3, z] + jnp.where(pore, FORCE_GAIN * (conc - REST_CONC), 0.0)
        base = 1.0 - 1.5 * (ux * ux + uy * uy + uz * uz)
        p = [out_pop[d, z] for d in range(19)]
        post = [None] * 19
        post[0] = jnp.where(pore, p[0] * (1 - OMEGA_FLOW) + (OMEGA_FLOW / 3.0) * rho * base, p[0])
        w1 = (OMEGA_FLOW / 18.0) * rho
        w2 = (OMEGA_FLOW / 36.0) * rho
        for d in range(1, 19, 2):
            o = OPP[d]
            along = None
            for c, u in zip(FLOW_DIRS[d], (ux, uy, uz)):
                if c:
                    along = (u if c > 0 else -u) if along is None else (along + u if c > 0 else along - u)
            w = w1 if d < 7 else w2
            even = base + 4.5 * along * along
            odd = 3.0 * along
            post[d] = jnp.where(pore, p[d] * (1 - OMEGA_FLOW) + w * (even + odd), p[d])
            post[o] = jnp.where(pore, p[o] * (1 - OMEGA_FLOW) + w * (even - odd), p[o])
        for d in range(19):
            F[d, z + 1] = post[d]
        return pack_flow(z, post, acc)

    def stream_flow(slot):
        def body(z, _):
            bits = B[z]
            pore = (bits & 1) != 0
            xz = x_planes([XC[0], XC[1]], z)
            moved = shifted_flow(slot, z, xz)
            here = [F[d, z + 1] for d in range(19)]
            p = [here[0]]
            for d in range(1, 19):
                p.append(jnp.where((bits & (1 << d)) != 0, moved[d], jnp.where(pore, here[OPP[d]], here[d])))
            for d in range(19):
                out_pop[d, z] = p[d]
            moments(z, p, jnp.where(pore, 1.0, 0.0))
            return 0
        lax.fori_loop(0, size_z, body, 0)

    def step(t, last):
        slot = lax.rem(t + 1, 2)
        acc = lax.fori_loop(0, size_z, collide_solute, zero2)
        for si in range(2):
            SM[0, si] = acc[si]
            SM[2, si] = S[5 + si, size_z if si == 0 else 1]
        exchange(solute_messages(), s_send, lambda k: s_recv.at[k])()
        S[5, 0] = SH[2, 0]
        S[6, size_z + 1] = SH[2, 1]
        finish_pack(lax.fori_loop(0, size_z, stream_solute_collide_flow, zero2))
        done = exchange(flow_messages(slot), f_send, lambda k: f_recv.at[slot, k])
        back = None
        if last:
            lax.fori_loop(0, comps, unplace, 0)
            back = exchange_blocks(stage2, recv2, b_send, b_recv, own_sem.at[1])
        done()
        flow_halo(slot)
        stream_flow(slot)
        return back

    lax.fori_loop(0, STEPS - 1, lambda t, _: (step(t, False), 0)[1], 0)
    back = step(jnp.int32(STEPS - 1), True)
    for c in back:
        c.wait()

    def deliver(c, _):
        for s in range(slots):
            T[c, s * rows:(s + 1) * rows, :] = choose(slot_where[s], pairs_of(recv2, c))
        for r in range(rows):
            out_sol[c, :, r * 128:(r + 1) * 128] = T[c, pl.ds(r, slots, stride=rows), :]
        return 0

    lax.fori_loop(0, comps, deliver, 0)


def shards(sizes, populations, solute_state, pore_mask, block_slot, slot_block):
    n_z = sizes[2]
    tiles = block_slot.shape[2]
    cap = -(-tiles // n_z)
    comps, slots, cells = solute_state.shape
    rows = cells // 128
    sz, sy, sx = pore_mask.shape
    f32 = jnp.float32
    blocks = pltpu.VMEM((n_z, cap, comps, rows, 128), f32)
    dma = pltpu.SemaphoreType.DMA
    vmem = pl.BlockSpec(memory_space=pltpu.VMEM)
    smem = pl.BlockSpec(memory_space=pltpu.SMEM)
    return pl.pallas_call(
        functools.partial(kernel, sizes, cap),
        out_shape=(
            jax.ShapeDtypeStruct(populations.shape, f32),
            jax.ShapeDtypeStruct(solute_state.shape, f32),
        ),
        in_specs=[vmem, vmem, vmem, smem, smem],
        out_specs=(vmem, vmem),
        scratch_shapes=[
            pltpu.VMEM((19, sz + 2, sy, sx), f32),
            pltpu.VMEM((7, sz, sy, sx), f32),
            pltpu.VMEM((7, sz + 2, sy, sx), f32),
            pltpu.VMEM((4, sz, sy, sx), f32),
            pltpu.VMEM((sz, sy, sx), jnp.int32),
            pltpu.VMEM((2, 16, 128), f32),
            pltpu.VMEM((2, 5, 16, 128), f32),
            pltpu.VMEM((2, 5, 16, 128), f32),
            pltpu.VMEM((2, 2, 5, 16, 128), f32),
            pltpu.VMEM((2, 2, 5, 16, 128), f32),
            pltpu.VMEM((2, 2, 2, 8, 128), f32),
            pltpu.VMEM((2, 2, 5, 16, 128), f32),
            pltpu.VMEM((2, 16, 128), f32),
            pltpu.VMEM((2, 2, 16, 128), f32),
            pltpu.VMEM((3, 2, 16, 128), f32),
            pltpu.VMEM((3, 2, 16, 128), f32),
            pltpu.VMEM((comps, slots * rows, 128), f32),
            blocks, blocks, blocks, blocks,
            dma((18,)), dma((2, 18)), dma((6,)), dma((6,)),
            dma((n_z,)), dma((n_z,)), dma((n_z,)), dma((n_z,)), dma((2,)),
        ],
        compiler_params=pltpu.CompilerParams(
            collective_id=0, has_side_effects=True, vmem_limit_bytes=40 * 1024 * 1024),
    )(populations, solute_state, pore_mask, block_slot, slot_block)


def solution(mesh):
    sizes = tuple(mesh.shape[a] for a in AXES)
    in_specs = (
        P(None, "gz", "gy", "gx"),
        P(None, ("gx", "gy", "gz"), None),
        P("gz", "gy", "gx"),
        P("gz", "gy", "gx"),
        P(("gx", "gy", "gz")),
    )
    out_specs = (P(None, "gz", "gy", "gx"), P(None, ("gx", "gy", "gz"), None))
    return jax.shard_map(
        functools.partial(shards, sizes), mesh=mesh, in_specs=in_specs, out_specs=out_specs, check_vma=False)
```

profile of v0, /device:TPU:8, one launch (start us, length us, event | category | flops | bytes accessed | tf_op | source)
XLA Modules:
  0.0 124.2 jit_solution(8159798886032434776)
XLA Ops:
  0.6 0.0 copy-start
  0.6 1.7 %copy-done = f32[19,16,16,128]{3,2,1,0:T(8,128)S(1)} copy-done((f32[19,16,16,128]{3,2,1,0:T(8,128)S(1)}, f32[19,16,16,128]{3,2,1,0:T(8,128)}, u32[]{:S(2)}) %copy-start) | copy-done | bytes 2490392
  2.3 0.0 copy-start.1
  2.3 1.2 copy-done.1
  3.5 0.0 copy-start.2
  3.5 0.9 copy-done.2
  4.4 0.0 copy-start.3
  4.4 0.7 copy-done.3
  5.1 0.0 copy-start.4
  5.1 0.7 copy-done.4
  5.7 116.1 %shard_map.68 = (f32[19,16,16,128]{3,2,1,0:T(8,128)S(1)}, f32[7,8,4096]{2,1,0:T(8,128)S(1)}) custom-call(f32[19,16,16,128]{3,2,1,0:T(8,128)S(1)} %copy-done, f32[7,8,4096]{2,1,0:T(8,128)S(1)} %copy-done.1, s32[16,16,128]{2,1,0:T(8,128)S(1)} %copy-done.2, s32[1,1,8]{2,1,0:T(1,128)S(1)} %copy-done.3, s32[8]{0:T(128)S(1)} %copy-done.4), custom_call_target="tpu_custom_call" | custom-call | tf_op jit(solution)/shard_map/pallas_call | solution.py:505
  121.8 1.5 %copy.9 = f32[19,16,16,128]{3,2,1,0:T(8,128)} copy(f32[19,16,16,128]{3,2,1,0:T(8,128)S(1)} %get-tuple-element.4) | data formatting | bytes 4980736
  123.2 0.9 copy.10
Async XLA Ops:
  0.6 1.7 %copy-start = (f32[19,16,16,128]{3,2,1,0:T(8,128)S(1)}, f32[19,16,16,128]{3,2,1,0:T(8,128)}, u32[]{:S(2)}) copy-start(f32[19,16,16,128]{3,2,1,0:T(8,128)} %pop_ref.1) | copy-start | bytes 7471108
  2.3 1.2 copy-start.1
  3.5 0.9 copy-start.2
  4.4 0.7 copy-start.3
  5.1 0.7 copy-start.4
where the time goes:
time: 124 us
  Pallas kernels  116 us (94%)
  local copies, waits for them, and re-layouts  7.46 us (6%)
    pallas_call x1, Pallas kernels, shards(): pl.pallas_call(functools.partial(kernel, sizes, cap), out_shape=(jax.Shap...  116 us
    unnamed x12, local copies, waits for them, and re-layouts  7.46 us

commit v1 on v0

--- a/solution.py
+++ b/solution.py
@@ -49,6 +49,17 @@
     return 0 if sign > 0 else 1
 
 
+UNROLL = 4
+
+
+def planes_loop(n, body, init):
+    def group(g, acc):
+        for k in range(UNROLL):
+            acc = body(g * UNROLL + k, acc)
+        return acc
+    return lax.fori_loop(0, n // UNROLL, group, init)
+
+
 def iota(axis, shape=(16, 128)):
     return lax.broadcasted_iota(jnp.int32, shape, axis)
 
@@ -70,12 +81,19 @@
 
 
 def kernel(
-    sizes, cap, pop_ref, sol_ref, mask_ref, bs_ref, sb_ref, out_pop, out_sol,
+    sizes, cap, pop_hbm, sol_hbm, mask_hbm, bs_ref, sb_ref, pop_out, sol_out,
+    out_pop, sol_ref, mask_ref,
     F, G, S, U, B, XM, YM, ZM, XH, YH, YE, ZH, XC, YC, SM, SH,
     T, stage, recv, stage2, recv2,
-    f_send, f_recv, s_send, s_recv, a_send, a_recv, b_send, b_recv, own_sem,
+    f_send, f_recv, s_send, s_recv, a_send, a_recv, b_send, b_recv, own_sem, io_sem,
 ):
     n_x, n_y, n_z = sizes
+    loads = [
+        pltpu.make_async_copy(src, dst, io_sem.at[k])
+        for k, (src, dst) in enumerate(((sol_hbm, sol_ref), (mask_hbm, mask_ref), (pop_hbm, out_pop)))
+    ]
+    for load in loads:
+        load.start()
     me = tuple(lax.axis_index(a) for a in AXES)
     lane = iota(1)
     row = iota(0)
@@ -165,6 +183,7 @@
             stage[q // cap, q % cap, c] = choose(slot_pick[q], blocks_of(c, slots))
         return 0
 
+    loads[0].wait()
     lax.fori_loop(0, comps, gather, 0)
     pl.semaphore_wait(barrier, count)
 
@@ -238,9 +257,9 @@
         for si, s in enumerate(SIGNS):
             w = None
             for j, v in enumerate(planes[si]):
-                r = pltpu.roll(v, 16 * j + 1 if s > 0 else 16 * j, 1) if (s > 0 or j) else v
+                r = pltpu.roll(v, z + (16 * j + 1 if s > 0 else 16 * j), 1)
                 w = r if w is None else jnp.where((lane >= 16 * j), r, w)
-            new.append(jnp.where(at_z, pltpu.roll(w, z, 1), acc[si]))
+            new.append(jnp.where(at_z, w, acc[si]))
         return tuple(new)
 
     def pack_flow(z, values, acc):
@@ -295,17 +314,13 @@
                 si = side(cx)
                 j = X_SIDE[si].index(d)
                 if cx > 0:
-                    h = pltpu.roll(xz[0], 128 - 16 * j, 1) if j else xz[0]
+                    h = pltpu.roll(xz[0], (128 - 16 * j) - z if j else lax.rem(128 - z, 128), 1)
                     v = jnp.where(lane == 0, h, pltpu.roll(v, 1, 1))
                 else:
-                    h = pltpu.roll(xz[1], 127 - 16 * j, 1)
+                    h = pltpu.roll(xz[1], (127 - 16 * j) - z, 1)
                     v = jnp.where(lane == 127, h, pltpu.roll(v, 127, 1))
             out.append(v)
         return out
-
-    def x_planes(refs, z):
-        back = lax.rem(128 - z, 128)
-        return [pltpu.roll(r, back, 1) for r in refs]
 
     def moments(z, p, porous):
         density = p[0]
@@ -324,22 +339,22 @@
         for ax in range(3):
             U[1 + ax, z] = m[ax]
 
+    loads[1].wait()
+    loads[2].wait()
+
     def fill(z, acc):
         porous = mask_ref[z].astype(jnp.float32)
         for d in range(19):
             F[d, z + 1] = porous
-        p = [pop_ref[d, z] for d in range(19)]
-        for d in range(19):
-            out_pop[d, z] = p[d]
-        moments(z, p, porous)
+        moments(z, [out_pop[d, z] for d in range(19)], porous)
         return pack_flow(z, [porous] * 19, acc)
 
-    finish_pack(lax.fori_loop(0, size_z, fill, zero2))
+    finish_pack(planes_loop(size_z, fill, zero2))
     exchange(flow_messages(0), f_send, lambda k: f_recv.at[0, k])()
     flow_halo(0)
 
     def link_bits(z, _):
-        xz = x_planes([XC[0], XC[1]], z)
+        xz = [XC[0], XC[1]]
         moved = shifted_flow(0, z, xz)
         pore = mask_ref[z] > 0
         bits = jnp.where(pore, 1, 0)
@@ -348,7 +363,7 @@
         B[z] = bits
         return 0
 
-    lax.fori_loop(0, size_z, link_bits, 0)
+    planes_loop(size_z, link_bits, 0)
 
     for c in moving:
         c.wait()
@@ -393,15 +408,15 @@
     def stream_solute_collide_flow(z, acc):
         bits = B[z]
         pore = (bits & 1) != 0
-        xz = x_planes([SH[0, 0], SH[0, 1]], z)
+        xz = [SH[0, 0], SH[0, 1]]
         s = [S[i, z + 1] for i in range(7)]
         new = [s[0]]
         for i in range(1, 7):
             cx, cy, cz = FLOW_DIRS[i]
             if cx > 0:
-                v = jnp.where(lane == 0, xz[0], pltpu.roll(s[i], 1, 1))
+                v = jnp.where(lane == 0, pltpu.roll(xz[0], lax.rem(128 - z, 128), 1), pltpu.roll(s[i], 1, 1))
             elif cx < 0:
-                v = jnp.where(lane == 127, pltpu.roll(xz[1], 127, 1), pltpu.roll(s[i], 127, 1))
+                v = jnp.where(lane == 127, pltpu.roll(xz[1], 127 - z, 1), pltpu.roll(s[i], 127, 1))
             elif cy:
                 e = SH[1, side(cy), pl.ds(z, 1), :]
                 v = jnp.where(row == (0 if cy > 0 else 15), jnp.broadcast_to(e, (16, 128)),
@@ -443,7 +458,7 @@
         def body(z, _):
             bits = B[z]
             pore = (bits & 1) != 0
-            xz = x_planes([XC[0], XC[1]], z)
+            xz = [XC[0], XC[1]]
             moved = shifted_flow(slot, z, xz)
             here = [F[d, z + 1] for d in range(19)]
             p = [here[0]]
@@ -453,18 +468,18 @@
                 out_pop[d, z] = p[d]
             moments(z, p, jnp.where(pore, 1.0, 0.0))
             return 0
-        lax.fori_loop(0, size_z, body, 0)
+        planes_loop(size_z, body, 0)
 
     def step(t, last):
         slot = lax.rem(t + 1, 2)
-        acc = lax.fori_loop(0, size_z, collide_solute, zero2)
+        acc = planes_loop(size_z, collide_solute, zero2)
         for si in range(2):
             SM[0, si] = acc[si]
             SM[2, si] = S[5 + si, size_z if si == 0 else 1]
         exchange(solute_messages(), s_send, lambda k: s_recv.at[k])()
         S[5, 0] = SH[2, 0]
         S[6, size_z + 1] = SH[2, 1]
-        finish_pack(lax.fori_loop(0, size_z, stream_solute_collide_flow, zero2))
+        finish_pack(planes_loop(size_z, stream_solute_collide_flow, zero2))
         done = exchange(flow_messages(slot), f_send, lambda k: f_recv.at[slot, k])
         back = None
         if last:
@@ -477,6 +492,8 @@
 
     lax.fori_loop(0, STEPS - 1, lambda t, _: (step(t, False), 0)[1], 0)
     back = step(jnp.int32(STEPS - 1), True)
+    store_pop = pltpu.make_async_copy(out_pop, pop_out, io_sem.at[3])
+    store_pop.start()
     for c in back:
         c.wait()
 
@@ -484,10 +501,14 @@
         for s in range(slots):
             T[c, s * rows:(s + 1) * rows, :] = choose(slot_where[s], pairs_of(recv2, c))
         for r in range(rows):
-            out_sol[c, :, r * 128:(r + 1) * 128] = T[c, pl.ds(r, slots, stride=rows), :]
+            sol_ref[c, :, r * 128:(r + 1) * 128] = T[c, pl.ds(r, slots, stride=rows), :]
         return 0
 
     lax.fori_loop(0, comps, deliver, 0)
+    store_sol = pltpu.make_async_copy(sol_ref, sol_out, io_sem.at[4])
+    store_sol.start()
+    store_pop.wait()
+    store_sol.wait()
 
 
 def shards(sizes, populations, solute_state, pore_mask, block_slot, slot_block):
@@ -500,7 +521,7 @@
     f32 = jnp.float32
     blocks = pltpu.VMEM((n_z, cap, comps, rows, 128), f32)
     dma = pltpu.SemaphoreType.DMA
-    vmem = pl.BlockSpec(memory_space=pltpu.VMEM)
+    hbm = pl.BlockSpec(memory_space=pl.ANY)
     smem = pl.BlockSpec(memory_space=pltpu.SMEM)
     return pl.pallas_call(
         functools.partial(kernel, sizes, cap),
@@ -508,9 +529,12 @@
             jax.ShapeDtypeStruct(populations.shape, f32),
             jax.ShapeDtypeStruct(solute_state.shape, f32),
         ),
-        in_specs=[vmem, vmem, vmem, smem, smem],
-        out_specs=(vmem, vmem),
+        in_specs=[hbm, hbm, hbm, smem, smem],
+        out_specs=(hbm, hbm),
         scratch_shapes=[
+            pltpu.VMEM(populations.shape, f32),
+            pltpu.VMEM(solute_state.shape, f32),
+            pltpu.VMEM(pore_mask.shape, jnp.int32),
             pltpu.VMEM((19, sz + 2, sy, sx), f32),
             pltpu.VMEM((7, sz, sy, sx), f32),
             pltpu.VMEM((7, sz + 2, sy, sx), f32),
@@ -530,10 +554,10 @@
             pltpu.VMEM((comps, slots * rows, 128), f32),
             blocks, blocks, blocks, blocks,
             dma((18,)), dma((2, 18)), dma((6,)), dma((6,)),
-            dma((n_z,)), dma((n_z,)), dma((n_z,)), dma((n_z,)), dma((2,)),
+            dma((n_z,)), dma((n_z,)), dma((n_z,)), dma((n_z,)), dma((2,)), dma((5,)),
         ],
         compiler_params=pltpu.CompilerParams(
-            collective_id=0, has_side_effects=True, vmem_limit_bytes=40 * 1024 * 1024),
+            collective_id=0, has_side_effects=True, vmem_limit_bytes=56 * 1024 * 1024),
     )(populations, solute_state, pore_mask, block_slot, slot_block)
 
 

time: 124 us -> 96.1 us (0.77)
  Pallas kernels: 116 us -> 90.9 us
  local copies, waits for them, and re-layouts: 7.46 us -> 4.38 us
    pallas_call x1, Pallas kernels: 116 us -> 90.9 us  [shards(): pl.pallas_call(functools.partial(kernel, sizes, cap), out_shape=(jax.Shap...]
    unnamed x12 -> x4, local copies, waits for them, and re-layouts: 7.46 us -> 4.38 us
where the time goes in v1:
time: 96.1 us; the launch traced here: 95.9 us
  Pallas kernels  90.9 us (95%)
  local copies, waits for them, and re-layouts  4.38 us (5%)
    pallas_call x1, Pallas kernels, shards(): pl.pallas_call(functools.partial(kernel, sizes, cap), out_shape=(jax.Shap...  90.9 us
    unnamed x4, local copies, waits for them, and re-layouts  4.38 us

profile of v1, /device:TPU:8, one launch (start us, length us, event | category | flops | bytes accessed | tf_op | source)
XLA Modules:
  0.0 95.9 jit_solution(15526502794891777634)
XLA Ops:
  0.6 90.9 %shard_map.68 = (f32[19,16,16,128]{3,2,1,0:T(8,128)}, f32[7,8,4096]{2,1,0:T(8,128)}) custom-call(f32[19,16,16,128]{3,2,1,0:T(8,128)} %pop_hbm.1, f32[7,8,4096]{2,1,0:T(8,128)} %sol_hbm.1, s32[16,16,128]{2,1,0:T(8,128)} %mask_hbm.1, s32[1,1,8]{2,1,0:T(1,128)} %bs_ref.1, s32[8]{0:T(128)} %sb_ref.1), custom_call_target="tpu_custom_call" | custom-call | tf_op jit(solution)/shard_map/pallas_call | solution.py:526
  91.5 0.0 copy-start
  91.5 3.4 %copy.9 = f32[19,16,16,128]{3,2,1,0:T(8,128)} copy(f32[19,16,16,128]{3,2,1,0:T(8,128)} %get-tuple-element.4) | data formatting | bytes 4980736
  95.0 0.0 copy-done
  95.0 0.9 copy.10
Async XLA Ops:
  91.5 3.5 %copy-start = (f32[7,8,4096]{2,1,0:T(8,128)S(1)}, f32[7,8,4096]{2,1,0:T(8,128)}, u32[]{:S(2)}) copy-start(f32[7,8,4096]{2,1,0:T(8,128)} %get-tuple-element.5) | copy-start | bytes 2752516

commit v2 on v1

--- a/solution.py
+++ b/solution.py
@@ -49,15 +49,12 @@
     return 0 if sign > 0 else 1
 
 
-UNROLL = 4
-
-
-def planes_loop(n, body, init):
+def planes_loop(n, body, init, first=0, unroll=4):
     def group(g, acc):
-        for k in range(UNROLL):
-            acc = body(g * UNROLL + k, acc)
+        for k in range(unroll):
+            acc = body(first + g * unroll + k, acc)
         return acc
-    return lax.fori_loop(0, n // UNROLL, group, init)
+    return lax.fori_loop(0, n // unroll, group, init)
 
 
 def iota(axis, shape=(16, 128)):
@@ -81,16 +78,17 @@
 
 
 def kernel(
-    sizes, cap, pop_hbm, sol_hbm, mask_hbm, bs_ref, sb_ref, pop_out, sol_out,
-    out_pop, sol_ref, mask_ref,
+    sizes, cap, pop_hbm, sol_hbm, mask_hbm, bs_hbm, sb_hbm, out_pop, out_sol,
+    sol_ref, mask_ref, bs_ref, sb_ref,
     F, G, S, U, B, XM, YM, ZM, XH, YH, YE, ZH, XC, YC, SM, SH,
     T, stage, recv, stage2, recv2,
-    f_send, f_recv, s_send, s_recv, a_send, a_recv, b_send, b_recv, own_sem, io_sem,
+    f_send, f_recv, s_send, s_recv, a_send, a_recv, b_send, b_recv, own_a, own_b, io_sem,
 ):
     n_x, n_y, n_z = sizes
     loads = [
         pltpu.make_async_copy(src, dst, io_sem.at[k])
-        for k, (src, dst) in enumerate(((sol_hbm, sol_ref), (mask_hbm, mask_ref), (pop_hbm, out_pop)))
+        for k, (src, dst) in enumerate((
+            (sb_hbm, sb_ref), (bs_hbm, bs_ref), (sol_hbm, sol_ref), (mask_hbm, mask_ref), (pop_hbm, out_pop)))
     ]
     for load in loads:
         load.start()
@@ -159,6 +157,8 @@
         where = [(group[s] * cap + rank[s] + 1) * held[s] - 1 for s in range(len(values))]
         return pick, where
 
+    loads[0].wait()
+    loads[1].wait()
     slot_pick, slot_where = routing([sb_ref[s] for s in range(slots)], tiles)
     tile_pick, tile_where = routing([bs_ref[0, 0, j] for j in range(tiles)], slots)
     rows = T.shape[1] // slots
@@ -167,7 +167,7 @@
         return [T[c, k * rows:(k + 1) * rows, :] for k in range(n)]
 
     def pairs_of(buf, c):
-        return [buf[q // cap, q % cap, c] for q in range(n_z * cap)]
+        return [buf[c, q // cap, q % cap] for q in range(n_z * cap)]
 
     def choose(index, options):
         at = jnp.full(options[0].shape, index, jnp.int32)
@@ -180,29 +180,36 @@
         for r in range(rows):
             T[c, pl.ds(r, slots, stride=rows), :] = sol_ref[c, :, r * 128:(r + 1) * 128]
         for q in range(n_z * cap):
-            stage[q // cap, q % cap, c] = choose(slot_pick[q], blocks_of(c, slots))
+            stage[c, q // cap, q % cap] = choose(slot_pick[q], blocks_of(c, slots))
         return 0
 
-    loads[0].wait()
+    loads[2].wait()
     lax.fori_loop(0, comps, gather, 0)
     pl.semaphore_wait(barrier, count)
 
-    def exchange_blocks(src, dst, send, rec, own):
+    hops = sorted(range(1, n_z), key=lambda k: abs(2 * k - n_z))
+
+    def block_copies(c, src, dst, send, rec, own):
         copies = []
-        for k in range(1, n_z):
+        for k in hops:
             other = lax.rem(me[2] + k, n_z)
             copies.append(pltpu.make_async_remote_copy(
-                src_ref=src.at[other], dst_ref=dst.at[me[2]],
-                send_sem=send.at[k], recv_sem=rec.at[k],
+                src_ref=src.at[c, other], dst_ref=dst.at[c, me[2]],
+                send_sem=send.at[k, c], recv_sem=rec.at[k, c],
                 device_id={"gx": me[0], "gy": me[1], "gz": other},
                 device_id_type=pl.DeviceIdType.MESH))
-        for c in copies:
-            c.start()
-        mine = pltpu.make_async_copy(src.at[me[2]], dst.at[me[2]], own)
-        mine.start()
-        return copies + [mine]
-
-    moving = exchange_blocks(stage, recv, a_send, a_recv, own_sem.at[0])
+        copies.append(pltpu.make_async_copy(src.at[c, me[2]], dst.at[c, me[2]], own.at[c]))
+        return copies
+
+    there = (stage, recv, a_send, a_recv, own_a)
+    back = (stage2, recv2, b_send, b_recv, own_b)
+
+    def send_blocks(c, _):
+        for copy in block_copies(c, *there):
+            copy.start()
+        return 0
+
+    lax.fori_loop(0, comps, send_blocks, 0)
 
     def flow_messages(slot):
         out = []
@@ -227,29 +234,36 @@
         return out
 
     def exchange(messages, send, rec):
-        copies = []
-        for k, (off, src, dst) in enumerate(messages):
-            copy = pltpu.make_async_remote_copy(
+        copies = [
+            pltpu.make_async_remote_copy(
                 src_ref=src, dst_ref=dst, send_sem=send.at[k], recv_sem=rec(k),
                 device_id=dev(off), device_id_type=pl.DeviceIdType.MESH)
-            copies.append(copy)
-
-            @pl.when(exists(off))
-            def _(copy=copy):
-                copy.start()
+            for k, (off, src, dst) in enumerate(messages)
+        ]
+
+        def start(which):
+            for (off, _, _), copy in zip(messages, copies):
+                if which(off):
+                    @pl.when(exists(off))
+                    def _(copy=copy):
+                        copy.start()
 
         def finish():
             for (off, _, _), copy in zip(messages, copies):
-                back = tuple(-o for o in off)
-
-                @pl.when(exists(back))
+                @pl.when(exists(tuple(-o for o in off)))
                 def _(copy=copy):
                     copy.wait_recv()
             for (off, _, _), copy in zip(messages, copies):
                 @pl.when(exists(off))
                 def _(copy=copy):
                     copy.wait_send()
-        return finish
+        return start, finish
+
+    def z_face(off):
+        return off[0] == 0 and off[1] == 0
+
+    def not_z_face(off):
+        return not z_face(off)
 
     def pack_x(z, planes, acc):
         new = []
@@ -269,9 +283,8 @@
                 YM[si, j, pl.ds(z, 1), :] = values[d][e:e + 1, :]
         return pack_x(z, [[values[d] for d in X_SIDE[si]] for si in range(2)], acc)
 
-    def finish_pack(acc):
+    def z_pack():
         for si, s in enumerate(SIGNS):
-            XM[si] = acc[si]
             for j, d in enumerate(Z_SIDE[si]):
                 ZM[si, j] = F[d, size_z if s > 0 else 1]
 
@@ -339,8 +352,8 @@
         for ax in range(3):
             U[1 + ax, z] = m[ax]
 
-    loads[1].wait()
-    loads[2].wait()
+    loads[3].wait()
+    loads[4].wait()
 
     def fill(z, acc):
         porous = mask_ref[z].astype(jnp.float32)
@@ -349,8 +362,11 @@
         moments(z, [out_pop[d, z] for d in range(19)], porous)
         return pack_flow(z, [porous] * 19, acc)
 
-    finish_pack(planes_loop(size_z, fill, zero2))
-    exchange(flow_messages(0), f_send, lambda k: f_recv.at[0, k])()
+    XM[0], XM[1] = planes_loop(size_z, fill, zero2)
+    z_pack()
+    start, finish = exchange(flow_messages(0), f_send, lambda k: f_recv.at[0, k])
+    start(lambda off: True)
+    finish()
     flow_halo(0)
 
     def link_bits(z, _):
@@ -365,10 +381,9 @@
 
     planes_loop(size_z, link_bits, 0)
 
-    for c in moving:
-        c.wait()
-
     def place(c, _):
+        for copy in block_copies(c, *there):
+            copy.wait()
         for j in range(tiles):
             T[c, j * rows:(j + 1) * rows, :] = choose(tile_where[j], pairs_of(recv, c))
         for r in range(rows):
@@ -382,7 +397,9 @@
         for r in range(rows):
             T[c, pl.ds(r, tiles, stride=rows), :] = swap_chunks(G[c, r // 2, (r % 2) * 8:(r % 2) * 8 + 8, :])
         for q in range(n_z * cap):
-            stage2[q // cap, q % cap, c] = choose(tile_pick[q], blocks_of(c, tiles))
+            stage2[c, q // cap, q % cap] = choose(tile_pick[q], blocks_of(c, tiles))
+        for copy in block_copies(c, *back):
+            copy.start()
         return 0
 
     def collide_solute(z, acc):
@@ -405,7 +422,7 @@
         return (jnp.where(at_z, pltpu.roll(post[1], z + 1, 1), acc[0]),
                 jnp.where(at_z, pltpu.roll(post[2], z, 1), acc[1]))
 
-    def stream_solute_collide_flow(z, acc):
+    def stream_solute(z, acc):
         bits = B[z]
         pore = (bits & 1) != 0
         xz = [SH[0, 0], SH[0, 1]]
@@ -424,11 +441,15 @@
             else:
                 v = S[i, z + (1 - cz)]
             new.append(jnp.where((bits & (1 << i)) != 0, v, jnp.where(pore, s[OPP[i]], s[i])))
+        for i in range(7):
+            G[i, z] = new[i]
+        return new
+
+    def collide_flow(z, acc, new):
+        pore = (B[z] & 1) != 0
         conc = new[0]
         for v in new[1:]:
             conc = conc + v
-        for i in range(7):
-            G[i, z] = new[i]
         rho = U[0, z]
         ux = U[1, z]
         uy = U[2, z]
@@ -470,45 +491,56 @@
             return 0
         planes_loop(size_z, body, 0)
 
+    ends = (0, size_z - 1)
+
     def step(t, last):
         slot = lax.rem(t + 1, 2)
-        acc = planes_loop(size_z, collide_solute, zero2)
+        start, finish = exchange(solute_messages(), s_send, lambda k: s_recv.at[k])
+        acc = zero2
+        for z in ends:
+            acc = collide_solute(z, acc)
         for si in range(2):
-            SM[0, si] = acc[si]
             SM[2, si] = S[5 + si, size_z if si == 0 else 1]
-        exchange(solute_messages(), s_send, lambda k: s_recv.at[k])()
+        start(z_face)
+        acc = planes_loop(size_z - 2, collide_solute, acc, 1, 7)
+        SM[0, 0], SM[0, 1] = acc
+        start(not_z_face)
+        finish()
         S[5, 0] = SH[2, 0]
         S[6, size_z + 1] = SH[2, 1]
-        finish_pack(planes_loop(size_z, stream_solute_collide_flow, zero2))
-        done = exchange(flow_messages(slot), f_send, lambda k: f_recv.at[slot, k])
-        back = None
         if last:
+            planes_loop(size_z, lambda z, _: (stream_solute(z, None), 0)[1], 0)
             lax.fori_loop(0, comps, unplace, 0)
-            back = exchange_blocks(stage2, recv2, b_send, b_recv, own_sem.at[1])
-        done()
+
+        def collide(z, acc):
+            new = [G[i, z] for i in range(7)] if last else stream_solute(z, None)
+            return collide_flow(z, acc, new)
+
+        start, finish = exchange(flow_messages(slot), f_send, lambda k: f_recv.at[slot, k])
+        acc = zero2
+        for z in ends:
+            acc = collide(z, acc)
+        z_pack()
+        start(z_face)
+        XM[0], XM[1] = planes_loop(size_z - 2, collide, acc, 1, 7)
+        start(not_z_face)
+        finish()
         flow_halo(slot)
         stream_flow(slot)
-        return back
 
     lax.fori_loop(0, STEPS - 1, lambda t, _: (step(t, False), 0)[1], 0)
-    back = step(jnp.int32(STEPS - 1), True)
-    store_pop = pltpu.make_async_copy(out_pop, pop_out, io_sem.at[3])
-    store_pop.start()
-    for c in back:
-        c.wait()
+    step(jnp.int32(STEPS - 1), True)
 
     def deliver(c, _):
+        for copy in block_copies(c, *back):
+            copy.wait()
         for s in range(slots):
             T[c, s * rows:(s + 1) * rows, :] = choose(slot_where[s], pairs_of(recv2, c))
         for r in range(rows):
-            sol_ref[c, :, r * 128:(r + 1) * 128] = T[c, pl.ds(r, slots, stride=rows), :]
+            out_sol[c, :, r * 128:(r + 1) * 128] = T[c, pl.ds(r, slots, stride=rows), :]
         return 0
 
     lax.fori_loop(0, comps, deliver, 0)
-    store_sol = pltpu.make_async_copy(sol_ref, sol_out, io_sem.at[4])
-    store_sol.start()
-    store_pop.wait()
-    store_sol.wait()
 
 
 def shards(sizes, populations, solute_state, pore_mask, block_slot, slot_block):
@@ -519,22 +551,23 @@
     rows = cells // 128
     sz, sy, sx = pore_mask.shape
     f32 = jnp.float32
-    blocks = pltpu.VMEM((n_z, cap, comps, rows, 128), f32)
+    blocks = pltpu.VMEM((comps, n_z, cap, rows, 128), f32)
     dma = pltpu.SemaphoreType.DMA
-    hbm = pl.BlockSpec(memory_space=pl.ANY)
-    smem = pl.BlockSpec(memory_space=pltpu.SMEM)
+    hbm = pl.BlockSpec(memory_space=pltpu.HBM)
+    vmem = pl.BlockSpec(memory_space=pltpu.VMEM)
     return pl.pallas_call(
         functools.partial(kernel, sizes, cap),
         out_shape=(
             jax.ShapeDtypeStruct(populations.shape, f32),
             jax.ShapeDtypeStruct(solute_state.shape, f32),
         ),
-        in_specs=[hbm, hbm, hbm, smem, smem],
-        out_specs=(hbm, hbm),
+        in_specs=[hbm] * 5,
+        out_specs=(vmem, vmem),
         scratch_shapes=[
-            pltpu.VMEM(populations.shape, f32),
             pltpu.VMEM(solute_state.shape, f32),
             pltpu.VMEM(pore_mask.shape, jnp.int32),
+            pltpu.SMEM(block_slot.shape, jnp.int32),
+            pltpu.SMEM(slot_block.shape, jnp.int32),
             pltpu.VMEM((19, sz + 2, sy, sx), f32),
             pltpu.VMEM((7, sz, sy, sx), f32),
             pltpu.VMEM((7, sz + 2, sy, sx), f32),
@@ -554,10 +587,11 @@
             pltpu.VMEM((comps, slots * rows, 128), f32),
             blocks, blocks, blocks, blocks,
             dma((18,)), dma((2, 18)), dma((6,)), dma((6,)),
-            dma((n_z,)), dma((n_z,)), dma((n_z,)), dma((n_z,)), dma((2,)), dma((5,)),
+            dma((n_z, comps)), dma((n_z, comps)), dma((n_z, comps)), dma((n_z, comps)),
+            dma((comps,)), dma((comps,)), dma((5,)),
         ],
         compiler_params=pltpu.CompilerParams(
-            collective_id=0, has_side_effects=True, vmem_limit_bytes=56 * 1024 * 1024),
+            collective_id=0, has_side_effects=True, vmem_limit_bytes=32 * 1024 * 1024),
     )(populations, solute_state, pore_mask, block_slot, slot_block)
 
 

time: 96.1 us -> 99.3 us (1.033)
  local copies, waits for them, and re-layouts: 4.38 us -> 7.46 us
    unnamed x4 -> x12, local copies, waits for them, and re-layouts: 4.38 us -> 7.46 us
where the time goes in v2:
time: 99.3 us; the launch traced here: 98.8 us
  Pallas kernels  90.7 us (91%)
  local copies, waits for them, and re-layouts  7.46 us (8%)
    pallas_call x1, Pallas kernels, shards(): pl.pallas_call(functools.partial(kernel, sizes, cap), out_shape=(jax.Shap...  90.7 us
    unnamed x12, local copies, waits for them, and re-layouts  7.46 us

profile of v2, /device:TPU:8, one launch (start us, length us, event | category | flops | bytes accessed | tf_op | source)
XLA Modules:
  0.0 98.8 jit_solution(17629972459093967333)
XLA Ops:
  0.6 0.0 copy-start
  0.6 1.7 %copy-done = f32[19,16,16,128]{3,2,1,0:T(8,128)S(1)} copy-done((f32[19,16,16,128]{3,2,1,0:T(8,128)S(1)}, f32[19,16,16,128]{3,2,1,0:T(8,128)}, u32[]{:S(2)}) %copy-start) | copy-done | bytes 2490392
  2.3 0.0 copy-start.1
  2.3 1.2 %copy-done.1 = f32[7,8,4096]{2,1,0:T(8,128)S(1)} copy-done((f32[7,8,4096]{2,1,0:T(8,128)S(1)}, f32[7,8,4096]{2,1,0:T(8,128)}, u32[]{:S(2)}) %copy-start.1) | copy-done | bytes 917528
  3.5 0.0 copy-start.2
  3.5 0.9 copy-done.2
  4.4 0.0 copy-start.3
  4.4 0.7 copy-done.3
  5.1 0.0 copy-start.4
  5.1 0.7 copy-done.4
  5.7 90.7 %shard_map.68 = (f32[19,16,16,128]{3,2,1,0:T(8,128)S(1)}, f32[7,8,4096]{2,1,0:T(8,128)S(1)}) custom-call(f32[19,16,16,128]{3,2,1,0:T(8,128)S(1)} %copy-done, f32[7,8,4096]{2,1,0:T(8,128)S(1)} %copy-done.1, s32[16,16,128]{2,1,0:T(8,128)S(1)} %copy-done.2, s32[1,1,8]{2,1,0:T(1,128)S(1)} %copy-done.3, s32[8]{0:T(128)S(1)} %copy-done.4), custom_call_target="tpu_custom_call" | custom-call | tf_op jit(solution)/shard_map/pallas_call | solution.py:558
  96.5 1.5 %copy.9 = f32[19,16,16,128]{3,2,1,0:T(8,128)} copy(f32[19,16,16,128]{3,2,1,0:T(8,128)S(1)} %get-tuple-element.4) | data formatting | bytes 4980736
  97.9 0.9 copy.10
Async XLA Ops:
  0.6 1.7 %copy-start = (f32[19,16,16,128]{3,2,1,0:T(8,128)S(1)}, f32[19,16,16,128]{3,2,1,0:T(8,128)}, u32[]{:S(2)}) copy-start(f32[19,16,16,128]{3,2,1,0:T(8,128)} %pop_hbm.1) | copy-start | bytes 7471108
  2.3 1.2 %copy-start.1 = (f32[7,8,4096]{2,1,0:T(8,128)S(1)}, f32[7,8,4096]{2,1,0:T(8,128)}, u32[]{:S(2)}) copy-start(f32[7,8,4096]{2,1,0:T(8,128)} %sol_hbm.1) | copy-start | bytes 2752516
  3.5 0.9 copy-start.2
  4.4 0.7 copy-start.3
  5.1 0.7 copy-start.4

commit v3 on v2

--- a/solution.py
+++ b/solution.py
@@ -78,11 +78,11 @@
 
 
 def kernel(
-    sizes, cap, pop_hbm, sol_hbm, mask_hbm, bs_hbm, sb_hbm, out_pop, out_sol,
-    sol_ref, mask_ref, bs_ref, sb_ref,
+    sizes, cap, pop_hbm, sol_hbm, mask_hbm, bs_hbm, sb_hbm, pop_out, sol_out,
+    out_pop, out_sol, sol_ref, mask_ref, bs_ref, sb_ref,
     F, G, S, U, B, XM, YM, ZM, XH, YH, YE, ZH, XC, YC, SM, SH,
     T, stage, recv, stage2, recv2,
-    f_send, f_recv, s_send, s_recv, a_send, a_recv, b_send, b_recv, own_a, own_b, io_sem,
+    f_send, f_recv, s_send, s_recv, a_send, a_recv, b_send, b_recv, own_a, own_b, io_sem, sol_sem,
 ):
     n_x, n_y, n_z = sizes
     loads = [
@@ -95,10 +95,13 @@
     me = tuple(lax.axis_index(a) for a in AXES)
     lane = iota(1)
     row = iota(0)
-    size_z = mask_ref.shape[0]
+    size_z = mask_ref.shape[0] // 16
     slots = sb_ref.shape[0]
     tiles = bs_ref.shape[2]
     comps = sol_ref.shape[0]
+
+    def rows_of(z):
+        return pl.ds(z * 16 if isinstance(z, int) else pl.multiple_of(z * 16, 16), 16)
 
     def exists(off):
         ok = None
@@ -290,10 +293,13 @@
 
     zero2 = (jnp.zeros((16, 128), jnp.float32),) * 2
 
-    def flow_halo(slot):
+    def z_halo(slot):
         for si, s in enumerate(SIGNS):
             for j, d in enumerate(Z_SIDE[si]):
                 F[d, 0 if s > 0 else size_z + 1] = ZH[slot, si, j]
+
+    def flow_halo(slot):
+        for si, s in enumerate(SIGNS):
             for zi, z in enumerate(SIGNS):
                 base = YH[slot, si, 3 + zi]
                 e = YE[slot, si, zi, 7:8, :] if z > 0 else YE[slot, si, zi, 0:1, :]
@@ -356,10 +362,10 @@
     loads[4].wait()
 
     def fill(z, acc):
-        porous = mask_ref[z].astype(jnp.float32)
+        porous = mask_ref[rows_of(z), :].astype(jnp.float32)
         for d in range(19):
             F[d, z + 1] = porous
-        moments(z, [out_pop[d, z] for d in range(19)], porous)
+        moments(z, [out_pop[d, rows_of(z), :] for d in range(19)], porous)
         return pack_flow(z, [porous] * 19, acc)
 
     XM[0], XM[1] = planes_loop(size_z, fill, zero2)
@@ -367,16 +373,17 @@
     start, finish = exchange(flow_messages(0), f_send, lambda k: f_recv.at[0, k])
     start(lambda off: True)
     finish()
+    z_halo(0)
     flow_halo(0)
 
     def link_bits(z, _):
         xz = [XC[0], XC[1]]
         moved = shifted_flow(0, z, xz)
-        pore = mask_ref[z] > 0
+        pore = mask_ref[rows_of(z), :] > 0
         bits = jnp.where(pore, 1, 0)
         for d in range(1, 19):
             bits = bits | jnp.where(jnp.logical_and(pore, moved[d] > 0.5), 1 << d, 0)
-        B[z] = bits
+        B[rows_of(z), :] = bits
         return 0
 
     planes_loop(size_z, link_bits, 0)
@@ -423,7 +430,7 @@
                 jnp.where(at_z, pltpu.roll(post[2], z, 1), acc[1]))
 
     def stream_solute(z, acc):
-        bits = B[z]
+        bits = B[rows_of(z), :]
         pore = (bits & 1) != 0
         xz = [SH[0, 0], SH[0, 1]]
         s = [S[i, z + 1] for i in range(7)]
@@ -446,7 +453,7 @@
         return new
 
     def collide_flow(z, acc, new):
-        pore = (B[z] & 1) != 0
+        pore = (B[rows_of(z), :] & 1) != 0
         conc = new[0]
         for v in new[1:]:
             conc = conc + v
@@ -455,7 +462,7 @@
         uy = U[2, z]
         uz = U[3, z] + jnp.where(pore, FORCE_GAIN * (conc - REST_CONC), 0.0)
         base = 1.0 - 1.5 * (ux * ux + uy * uy + uz * uz)
-        p = [out_pop[d, z] for d in range(19)]
+        p = [out_pop[d, rows_of(z), :] for d in range(19)]
         post = [None] * 19
         post[0] = jnp.where(pore, p[0] * (1 - OMEGA_FLOW) + (OMEGA_FLOW / 3.0) * rho * base, p[0])
         w1 = (OMEGA_FLOW / 18.0) * rho
@@ -475,36 +482,70 @@
             F[d, z + 1] = post[d]
         return pack_flow(z, post, acc)
 
-    def stream_flow(slot):
-        def body(z, _):
-            bits = B[z]
-            pore = (bits & 1) != 0
-            xz = [XC[0], XC[1]]
-            moved = shifted_flow(slot, z, xz)
-            here = [F[d, z + 1] for d in range(19)]
-            p = [here[0]]
-            for d in range(1, 19):
-                p.append(jnp.where((bits & (1 << d)) != 0, moved[d], jnp.where(pore, here[OPP[d]], here[d])))
-            for d in range(19):
-                out_pop[d, z] = p[d]
-            moments(z, p, jnp.where(pore, 1.0, 0.0))
-            return 0
-        planes_loop(size_z, body, 0)
-
-    ends = (0, size_z - 1)
+    def shift_in_plane(d, v):
+        cx, cy, _ = FLOW_DIRS[d]
+        if cy:
+            v = pltpu.roll(v, 1 if cy > 0 else 15, 0)
+        if cx:
+            v = pltpu.roll(v, 1 if cx > 0 else 127, 1)
+        return v
+
+    def stream_inside(z, _):
+        bits = B[rows_of(z), :]
+        pore = (bits & 1) != 0
+        here = [F[d, z + 1] for d in range(19)]
+        out_pop[0, rows_of(z), :] = here[0]
+        for d in range(1, 19):
+            cz = FLOW_DIRS[d][2]
+            v = shift_in_plane(d, F[d, z + (1 - cz)] if cz else here[d])
+            out_pop[d, rows_of(z), :] = jnp.where(
+                (bits & (1 << d)) != 0, v, jnp.where(pore, here[OPP[d]], here[d]))
+        return 0
+
+    def edges_yz(slot):
+        for si, s in enumerate(SIGNS):
+            z = 0 if s > 0 else size_z - 1
+            bits = B[rows_of(z), :]
+            for j, d in enumerate(Z_SIDE[si]):
+                v = shift_in_plane(d, ZH[slot, si, j])
+                out_pop[d, rows_of(z), :] = jnp.where((bits & (1 << d)) != 0, v, out_pop[d, rows_of(z), :])
+        for si, s in enumerate(SIGNS):
+            at = pl.ds(0 if s > 0 else 15, size_z, stride=16)
+            bits = B[at, :]
+            for j, d in enumerate(Y_SIDE[si]):
+                cx = FLOW_DIRS[d][0]
+                v = YH[slot, si, j] if j < 3 else YC[si, j - 3]
+                if cx:
+                    v = pltpu.roll(v, 1 if cx > 0 else 127, 1)
+                out_pop[d, at, :] = jnp.where((bits & (1 << d)) != 0, v, out_pop[d, at, :])
+
+    def edge_x(z):
+        bits = B[rows_of(z), :]
+        p = [out_pop[d, rows_of(z), :] for d in range(19)]
+        for si, s in enumerate(SIGNS):
+            edge = jnp.where(lane == (0 if s > 0 else 127), bits, 0)
+            for j, d in enumerate(X_SIDE[si]):
+                back = (128 if s > 0 else 127) - 16 * j - z
+                if s > 0 and j == 0:
+                    back = lax.rem(back, 128)
+                p[d] = jnp.where((edge & (1 << d)) != 0, pltpu.roll(XC[si], back, 1), p[d])
+                out_pop[d, rows_of(z), :] = p[d]
+        return p, bits
+
+    def edge_x_collide(z, acc):
+        p, bits = edge_x(z)
+        moments(z, p, jnp.where((bits & 1) != 0, 1.0, 0.0))
+        return collide_solute(z, acc)
+
+    def solute_post(body):
+        SM[0, 0], SM[0, 1] = planes_loop(size_z, body, zero2)
+        for si in range(2):
+            SM[2, si] = S[5 + si, size_z if si == 0 else 1]
 
     def step(t, last):
         slot = lax.rem(t + 1, 2)
         start, finish = exchange(solute_messages(), s_send, lambda k: s_recv.at[k])
-        acc = zero2
-        for z in ends:
-            acc = collide_solute(z, acc)
-        for si in range(2):
-            SM[2, si] = S[5 + si, size_z if si == 0 else 1]
-        start(z_face)
-        acc = planes_loop(size_z - 2, collide_solute, acc, 1, 7)
-        SM[0, 0], SM[0, 1] = acc
-        start(not_z_face)
+        start(lambda off: True)
         finish()
         S[5, 0] = SH[2, 0]
         S[6, size_z + 1] = SH[2, 1]
@@ -516,20 +557,25 @@
             new = [G[i, z] for i in range(7)] if last else stream_solute(z, None)
             return collide_flow(z, acc, new)
 
+        XM[0], XM[1] = planes_loop(size_z, collide, zero2)
+        z_pack()
         start, finish = exchange(flow_messages(slot), f_send, lambda k: f_recv.at[slot, k])
-        acc = zero2
-        for z in ends:
-            acc = collide(z, acc)
-        z_pack()
         start(z_face)
-        XM[0], XM[1] = planes_loop(size_z - 2, collide, acc, 1, 7)
         start(not_z_face)
+        planes_loop(size_z, stream_inside, 0)
         finish()
         flow_halo(slot)
-        stream_flow(slot)
-
+        edges_yz(slot)
+        if last:
+            planes_loop(size_z, lambda z, _: (edge_x(z), 0)[1], 0)
+        else:
+            solute_post(edge_x_collide)
+
+    solute_post(collide_solute)
     lax.fori_loop(0, STEPS - 1, lambda t, _: (step(t, False), 0)[1], 0)
     step(jnp.int32(STEPS - 1), True)
+    store_pop = pltpu.make_async_copy(out_pop, pop_out, io_sem.at[5])
+    store_pop.start()
 
     def deliver(c, _):
         for copy in block_copies(c, *back):
@@ -538,9 +584,13 @@
             T[c, s * rows:(s + 1) * rows, :] = choose(slot_where[s], pairs_of(recv2, c))
         for r in range(rows):
             out_sol[c, :, r * 128:(r + 1) * 128] = T[c, pl.ds(r, slots, stride=rows), :]
+        pltpu.make_async_copy(out_sol.at[c], sol_out.at[c], sol_sem.at[c]).start()
         return 0
 
     lax.fori_loop(0, comps, deliver, 0)
+    for c in range(comps):
+        pltpu.make_async_copy(out_sol.at[c], sol_out.at[c], sol_sem.at[c]).wait()
+    store_pop.wait()
 
 
 def shards(sizes, populations, solute_state, pore_mask, block_slot, slot_block):
@@ -553,26 +603,27 @@
     f32 = jnp.float32
     blocks = pltpu.VMEM((comps, n_z, cap, rows, 128), f32)
     dma = pltpu.SemaphoreType.DMA
-    hbm = pl.BlockSpec(memory_space=pltpu.HBM)
-    vmem = pl.BlockSpec(memory_space=pltpu.VMEM)
-    return pl.pallas_call(
+    hbm = pl.BlockSpec(memory_space=pl.ANY)
+    new_populations, new_solute = pl.pallas_call(
         functools.partial(kernel, sizes, cap),
         out_shape=(
-            jax.ShapeDtypeStruct(populations.shape, f32),
+            jax.ShapeDtypeStruct((19, sz * sy, sx), f32),
             jax.ShapeDtypeStruct(solute_state.shape, f32),
         ),
         in_specs=[hbm] * 5,
-        out_specs=(vmem, vmem),
+        out_specs=(hbm, hbm),
         scratch_shapes=[
+            pltpu.VMEM((19, sz * sy, sx), f32),
             pltpu.VMEM(solute_state.shape, f32),
-            pltpu.VMEM(pore_mask.shape, jnp.int32),
+            pltpu.VMEM(solute_state.shape, f32),
+            pltpu.VMEM((sz * sy, sx), jnp.int32),
             pltpu.SMEM(block_slot.shape, jnp.int32),
             pltpu.SMEM(slot_block.shape, jnp.int32),
             pltpu.VMEM((19, sz + 2, sy, sx), f32),
             pltpu.VMEM((7, sz, sy, sx), f32),
             pltpu.VMEM((7, sz + 2, sy, sx), f32),
             pltpu.VMEM((4, sz, sy, sx), f32),
-            pltpu.VMEM((sz, sy, sx), jnp.int32),
+            pltpu.VMEM((sz * sy, sx), jnp.int32),
             pltpu.VMEM((2, 16, 128), f32),
             pltpu.VMEM((2, 5, 16, 128), f32),
             pltpu.VMEM((2, 5, 16, 128), f32),
@@ -588,11 +639,12 @@
             blocks, blocks, blocks, blocks,
             dma((18,)), dma((2, 18)), dma((6,)), dma((6,)),
             dma((n_z, comps)), dma((n_z, comps)), dma((n_z, comps)), dma((n_z, comps)),
-            dma((comps,)), dma((comps,)), dma((5,)),
+            dma((comps,)), dma((comps,)), dma((6,)), dma((comps,)),
         ],
         compiler_params=pltpu.CompilerParams(
-            collective_id=0, has_side_effects=True, vmem_limit_bytes=32 * 1024 * 1024),
-    )(populations, solute_state, pore_mask, block_slot, slot_block)
+            collective_id=0, has_side_effects=True, vmem_limit_bytes=56 * 1024 * 1024),
+    )(populations.reshape(19, sz * sy, sx), solute_state, pore_mask.reshape(sz * sy, sx), block_slot, slot_block)
+    return new_populations.reshape(populations.shape), new_solute
 
 
 def solution(mesh):

time: 99.3 us -> 95.5 us (0.962)
  local copies, waits for them, and re-layouts: 7.46 us -> 4.38 us
    unnamed x12 -> x4, local copies, waits for them, and re-layouts: 7.46 us -> 4.38 us
where the time goes in v3:
time: 95.5 us; the launch traced here: 95.3 us
  Pallas kernels  90.3 us (95%)
  local copies, waits for them, and re-layouts  4.38 us (5%)
    pallas_call x1, Pallas kernels, shards(): pl.pallas_call(functools.partial(kernel, sizes, cap), out_shape=(jax.Shap...  90.3 us
    unnamed x4, local copies, waits for them, and re-layouts  4.38 us

profile of v3, /device:TPU:8, one launch (start us, length us, event | category | flops | bytes accessed | tf_op | source)
XLA Modules:
  0.0 95.3 jit_solution(2930531541825994029)
XLA Ops:
  0.6 90.3 %shard_map.68 = (f32[19,256,128]{2,1,0:T(8,128)}, f32[7,8,4096]{2,1,0:T(8,128)}) custom-call(f32[19,256,128]{2,1,0:T(8,128)} %bitcast.4, f32[7,8,4096]{2,1,0:T(8,128)} %sol_hbm.1, s32[256,128]{1,0:T(8,128)} %bitcast.5, s32[1,1,8]{2,1,0:T(1,128)} %bs_hbm.1, s32[8]{0:T(128)} %sb_hbm.1), custom_call_target="tpu_custom_call" | custom-call | tf_op jit(solution)/shard_map/pallas_call | solution.py:607
  90.9 0.0 copy-start
  91.0 3.4 %copy.9 = f32[19,16,16,128]{3,2,1,0:T(8,128)} copy(f32[19,16,16,128]{3,2,1,0:T(8,128)} %bitcast.3) | data formatting | bytes 4980736
  94.4 0.0 copy-done
  94.4 0.9 copy.10
Async XLA Ops:
  90.9 3.5 %copy-start = (f32[7,8,4096]{2,1,0:T(8,128)S(1)}, f32[7,8,4096]{2,1,0:T(8,128)}, u32[]{:S(2)}) copy-start(f32[7,8,4096]{2,1,0:T(8,128)} %get-tuple-element.9) | copy-start | bytes 2752516

commit v4 on v3

--- a/solution.py
+++ b/solution.py
@@ -82,7 +82,7 @@
     out_pop, out_sol, sol_ref, mask_ref, bs_ref, sb_ref,
     F, G, S, U, B, XM, YM, ZM, XH, YH, YE, ZH, XC, YC, SM, SH,
     T, stage, recv, stage2, recv2,
-    f_send, f_recv, s_send, s_recv, a_send, a_recv, b_send, b_recv, own_a, own_b, io_sem, sol_sem,
+    f_send, f_recv, s_send, s_recv, a_send, a_recv, b_send, b_recv, own_sem, io_sem, sol_sem,
 ):
     n_x, n_y, n_z = sizes
     loads = [
@@ -170,7 +170,7 @@
         return [T[c, k * rows:(k + 1) * rows, :] for k in range(n)]
 
     def pairs_of(buf, c):
-        return [buf[c, q // cap, q % cap] for q in range(n_z * cap)]
+        return [buf[q // cap, q % cap, c] for q in range(n_z * cap)]
 
     def choose(index, options):
         at = jnp.full(options[0].shape, index, jnp.int32)
@@ -183,7 +183,7 @@
         for r in range(rows):
             T[c, pl.ds(r, slots, stride=rows), :] = sol_ref[c, :, r * 128:(r + 1) * 128]
         for q in range(n_z * cap):
-            stage[c, q // cap, q % cap] = choose(slot_pick[q], blocks_of(c, slots))
+            stage[q // cap, q % cap, c] = choose(slot_pick[q], blocks_of(c, slots))
         return 0
 
     loads[2].wait()
@@ -192,27 +192,22 @@
 
     hops = sorted(range(1, n_z), key=lambda k: abs(2 * k - n_z))
 
-    def block_copies(c, src, dst, send, rec, own):
+    def block_copies(src, dst, send, rec, own):
         copies = []
         for k in hops:
             other = lax.rem(me[2] + k, n_z)
             copies.append(pltpu.make_async_remote_copy(
-                src_ref=src.at[c, other], dst_ref=dst.at[c, me[2]],
-                send_sem=send.at[k, c], recv_sem=rec.at[k, c],
+                src_ref=src.at[other], dst_ref=dst.at[me[2]],
+                send_sem=send.at[k], recv_sem=rec.at[k],
                 device_id={"gx": me[0], "gy": me[1], "gz": other},
                 device_id_type=pl.DeviceIdType.MESH))
-        copies.append(pltpu.make_async_copy(src.at[c, me[2]], dst.at[c, me[2]], own.at[c]))
+        copies.append(pltpu.make_async_copy(src.at[me[2]], dst.at[me[2]], own))
         return copies
 
-    there = (stage, recv, a_send, a_recv, own_a)
-    back = (stage2, recv2, b_send, b_recv, own_b)
-
-    def send_blocks(c, _):
-        for copy in block_copies(c, *there):
-            copy.start()
-        return 0
-
-    lax.fori_loop(0, comps, send_blocks, 0)
+    there = block_copies(stage, recv, a_send, a_recv, own_sem.at[0])
+    back = block_copies(stage2, recv2, b_send, b_recv, own_sem.at[1])
+    for copy in there:
+        copy.start()
 
     def flow_messages(slot):
         out = []
@@ -388,9 +383,10 @@
 
     planes_loop(size_z, link_bits, 0)
 
+    for copy in there:
+        copy.wait()
+
     def place(c, _):
-        for copy in block_copies(c, *there):
-            copy.wait()
         for j in range(tiles):
             T[c, j * rows:(j + 1) * rows, :] = choose(tile_where[j], pairs_of(recv, c))
         for r in range(rows):
@@ -404,9 +400,7 @@
         for r in range(rows):
             T[c, pl.ds(r, tiles, stride=rows), :] = swap_chunks(G[c, r // 2, (r % 2) * 8:(r % 2) * 8 + 8, :])
         for q in range(n_z * cap):
-            stage2[c, q // cap, q % cap] = choose(tile_pick[q], blocks_of(c, tiles))
-        for copy in block_copies(c, *back):
-            copy.start()
+            stage2[q // cap, q % cap, c] = choose(tile_pick[q], blocks_of(c, tiles))
         return 0
 
     def collide_solute(z, acc):
@@ -549,19 +543,19 @@
         finish()
         S[5, 0] = SH[2, 0]
         S[6, size_z + 1] = SH[2, 1]
-        if last:
-            planes_loop(size_z, lambda z, _: (stream_solute(z, None), 0)[1], 0)
-            lax.fori_loop(0, comps, unplace, 0)
 
         def collide(z, acc):
-            new = [G[i, z] for i in range(7)] if last else stream_solute(z, None)
-            return collide_flow(z, acc, new)
+            return collide_flow(z, acc, stream_solute(z, None))
 
         XM[0], XM[1] = planes_loop(size_z, collide, zero2)
         z_pack()
         start, finish = exchange(flow_messages(slot), f_send, lambda k: f_recv.at[slot, k])
         start(z_face)
         start(not_z_face)
+        if last:
+            lax.fori_loop(0, comps, unplace, 0)
+            for copy in back:
+                copy.start()
         planes_loop(size_z, stream_inside, 0)
         finish()
         flow_halo(slot)
@@ -577,9 +571,10 @@
     store_pop = pltpu.make_async_copy(out_pop, pop_out, io_sem.at[5])
     store_pop.start()
 
+    for copy in back:
+        copy.wait()
+
     def deliver(c, _):
-        for copy in block_copies(c, *back):
-            copy.wait()
         for s in range(slots):
             T[c, s * rows:(s + 1) * rows, :] = choose(slot_where[s], pairs_of(recv2, c))
         for r in range(rows):
@@ -601,7 +596,7 @@
     rows = cells // 128
     sz, sy, sx = pore_mask.shape
     f32 = jnp.float32
-    blocks = pltpu.VMEM((comps, n_z, cap, rows, 128), f32)
+    blocks = pltpu.VMEM((n_z, cap, comps, rows, 128), f32)
     dma = pltpu.SemaphoreType.DMA
     hbm = pl.BlockSpec(memory_space=pl.ANY)
     new_populations, new_solute = pl.pallas_call(
@@ -638,8 +633,7 @@
             pltpu.VMEM((comps, slots * rows, 128), f32),
             blocks, blocks, blocks, blocks,
             dma((18,)), dma((2, 18)), dma((6,)), dma((6,)),
-            dma((n_z, comps)), dma((n_z, comps)), dma((n_z, comps)), dma((n_z, comps)),
-            dma((comps,)), dma((comps,)), dma((6,)), dma((comps,)),
+            dma((n_z,)), dma((n_z,)), dma((n_z,)), dma((n_z,)), dma((2,)), dma((6,)), dma((comps,)),
         ],
         compiler_params=pltpu.CompilerParams(
             collective_id=0, has_side_effects=True, vmem_limit_bytes=56 * 1024 * 1024),

time: 95.5 us -> 95 us (level)
  no operation moved by 1% of the time
where the time goes in v4:
time: 95 us; the launch traced here: 94.8 us
  Pallas kernels  89.8 us (95%)
  local copies, waits for them, and re-layouts  4.38 us (5%)
    pallas_call x1, Pallas kernels, shards(): pl.pallas_call(functools.partial(kernel, sizes, cap), out_shape=(jax.Shap...  89.8 us
    unnamed x4, local copies, waits for them, and re-layouts  4.38 us

profile of v4, /device:TPU:8, one launch (start us, length us, event | category | flops | bytes accessed | tf_op | source)
XLA Modules:
  0.0 94.8 jit_solution(8545211120203283496)
XLA Ops:
  0.6 89.8 %shard_map.68 = (f32[19,256,128]{2,1,0:T(8,128)}, f32[7,8,4096]{2,1,0:T(8,128)}) custom-call(f32[19,256,128]{2,1,0:T(8,128)} %bitcast.4, f32[7,8,4096]{2,1,0:T(8,128)} %sol_hbm.1, s32[256,128]{1,0:T(8,128)} %bitcast.5, s32[1,1,8]{2,1,0:T(1,128)} %bs_hbm.1, s32[8]{0:T(128)} %sb_hbm.1), custom_call_target="tpu_custom_call" | custom-call | tf_op jit(solution)/shard_map/pallas_call | solution.py:602
  90.4 0.0 copy-start
  90.4 3.4 %copy.9 = f32[19,16,16,128]{3,2,1,0:T(8,128)} copy(f32[19,16,16,128]{3,2,1,0:T(8,128)} %bitcast.3) | data formatting | bytes 4980736
  93.8 0.0 copy-done
  93.9 0.9 copy.10
Async XLA Ops:
  90.4 3.5 %copy-start = (f32[7,8,4096]{2,1,0:T(8,128)S(1)}, f32[7,8,4096]{2,1,0:T(8,128)}, u32[]{:S(2)}) copy-start(f32[7,8,4096]{2,1,0:T(8,128)} %get-tuple-element.9) | copy-start | bytes 2752516

commit v5 on v4

--- a/solution.py
+++ b/solution.py
@@ -188,7 +188,6 @@
 
     loads[2].wait()
     lax.fori_loop(0, comps, gather, 0)
-    pl.semaphore_wait(barrier, count)
 
     hops = sorted(range(1, n_z), key=lambda k: abs(2 * k - n_z))
 
@@ -206,9 +205,6 @@
 
     there = block_copies(stage, recv, a_send, a_recv, own_sem.at[0])
     back = block_copies(stage2, recv2, b_send, b_recv, own_sem.at[1])
-    for copy in there:
-        copy.start()
-
     def flow_messages(slot):
         out = []
         for si, s in enumerate(SIGNS):
@@ -354,19 +350,28 @@
             U[1 + ax, z] = m[ax]
 
     loads[3].wait()
-    loads[4].wait()
 
     def fill(z, acc):
         porous = mask_ref[rows_of(z), :].astype(jnp.float32)
         for d in range(19):
             F[d, z + 1] = porous
-        moments(z, [out_pop[d, rows_of(z), :] for d in range(19)], porous)
         return pack_flow(z, [porous] * 19, acc)
 
     XM[0], XM[1] = planes_loop(size_z, fill, zero2)
     z_pack()
     start, finish = exchange(flow_messages(0), f_send, lambda k: f_recv.at[0, k])
-    start(lambda off: True)
+    pl.semaphore_wait(barrier, count)
+    start(z_face)
+    start(not_z_face)
+    for copy in there:
+        copy.start()
+    loads[4].wait()
+
+    def first_moments(z, _):
+        moments(z, [out_pop[d, rows_of(z), :] for d in range(19)], mask_ref[rows_of(z), :].astype(jnp.float32))
+        return 0
+
+    planes_loop(size_z, first_moments, 0)
     finish()
     z_halo(0)
     flow_halo(0)

time: 95 us -> 93.9 us (0.988)
  Pallas kernels: 89.8 us -> 88.7 us
    pallas_call x1, Pallas kernels: 89.8 us -> 88.7 us  [shards(): pl.pallas_call(functools.partial(kernel, sizes, cap), out_shape=(jax.Shap...]
where the time goes in v5:
time: 93.9 us; the launch traced here: 93.7 us
  Pallas kernels  88.7 us (94%)
  local copies, waits for them, and re-layouts  4.38 us (5%)
    pallas_call x1, Pallas kernels, shards(): pl.pallas_call(functools.partial(kernel, sizes, cap), out_shape=(jax.Shap...  88.7 us
    unnamed x4, local copies, waits for them, and re-layouts  4.38 us

profile of v5, /device:TPU:8, one launch (start us, length us, event | category | flops | bytes accessed | tf_op | source)
XLA Modules:
  0.0 93.7 jit_solution(2570338294927586527)
XLA Ops:
  0.6 88.7 %shard_map.68 = (f32[19,256,128]{2,1,0:T(8,128)}, f32[7,8,4096]{2,1,0:T(8,128)}) custom-call(f32[19,256,128]{2,1,0:T(8,128)} %bitcast.4, f32[7,8,4096]{2,1,0:T(8,128)} %sol_hbm.1, s32[256,128]{1,0:T(8,128)} %bitcast.5, s32[1,1,8]{2,1,0:T(1,128)} %bs_hbm.1, s32[8]{0:T(128)} %sb_hbm.1), custom_call_target="tpu_custom_call" | custom-call | tf_op jit(solution)/shard_map/pallas_call | solution.py:607
  89.3 0.0 copy-start
  89.4 3.4 %copy.9 = f32[19,16,16,128]{3,2,1,0:T(8,128)} copy(f32[19,16,16,128]{3,2,1,0:T(8,128)} %bitcast.3) | data formatting | bytes 4980736
  92.8 0.0 copy-done
  92.8 0.9 copy.10
Async XLA Ops:
  89.3 3.5 %copy-start = (f32[7,8,4096]{2,1,0:T(8,128)S(1)}, f32[7,8,4096]{2,1,0:T(8,128)}, u32[]{:S(2)}) copy-start(f32[7,8,4096]{2,1,0:T(8,128)} %get-tuple-element.9) | copy-start | bytes 2752516
